TPU v7x, 512 devices: a whole 4x8x8 slice. The times are simulated.
512 devices in a mesh: ep: 32 (over x_lo, z, core), et: 16 (over x_hi, y).
Axes of the slice: x: 4 (x_hi: 2, x_lo: 2; x = x_hi * 2 + x_lo), y: 8, z: 8, core: 2. Of those that a mesh axis runs over, the one named last changes fastest.
Arguments:
- tokens: bfloat16 [8192, 2048], P('ep', 'et'), may hold values from -6 to 6
- cotangent: bfloat16 [8192, 2048], P('ep', 'et'), may hold values from -1.5 to 1.5
- w_up: bfloat16 [32, 2048, 4096], P('ep', None, 'et'), may hold values from -0.1875 to 0.1875
- w_down: bfloat16 [32, 4096, 2048], P('ep', 'et'), may hold values from -0.09375 to 0.09375
- saved_pre: bfloat16 [32, 512, 4096], P('ep', None, 'et'), may hold values from -6 to 6
- gates: float32 [32, 512], P('ep'), may hold values from 0.25 to 2
- picks: int32 [32, 32, 16], P('ep'), may hold values from 0 to 255, as said below
- counts: int32 [32, 32], P('ep'), may hold values from 4 to 16, as said below
Outputs:
- grad_tokens: bfloat16 [8192, 2048], P('ep', 'et')
- grad_up: bfloat16 [32, 2048, 4096], P('ep', None, 'et')
- grad_down: bfloat16 [32, 4096, 2048], P('ep', 'et')
- gate_grad: float32 [32, 512], P('ep')
Inputs may be any that keep to these rules, and one draw needn't show every extreme that they name: For each ep index s and expert e the entries picks[s, e, :] are distinct tokens among that index's 256; slots k >= counts[s, e] are padding and are ignored. `counts`: some expert takes 16 tokens from every ep index.
All inputs are finite; a program needn't handle non-finite values.
Results may differ from a plain program's by a relative error of at most 0.0049.
Values may be sent and summed in bfloat16 or wider, within the bound.
No kernel may reach another device: no remote copies, remote signals or barrier semaphores. Data moves between devices by JAX's collectives and lax.ppermute only.
A program may use at most 64 MiB of HBM per device.

v0:
```python
import jax
import jax.numpy as jnp
from jax import lax
from jax.sharding import PartitionSpec as P


def per_device(tokens, cotangent, w_up, w_down, saved_pre, gates, picks, counts):
    local_idx = picks[0]
    n_experts, n_slots = local_idx.shape
    n_tokens = tokens.shape[0]
    slot_kept = lax.broadcasted_iota(jnp.int32, (n_experts, n_slots), 1) < counts[0][:, None]
    flat_idx = local_idx.reshape(-1)
    bf_zero = jnp.zeros((), tokens.dtype)
    picked_x = jnp.take(tokens, flat_idx, axis=0).reshape(n_experts, n_slots, -1)
    picked_y = jnp.take(cotangent, flat_idx, axis=0).reshape(n_experts, n_slots, -1)
    picked_x = jnp.where(slot_kept[:, :, None], picked_x, bf_zero)
    picked_y = jnp.where(slot_kept[:, :, None], picked_y, bf_zero)
    arrived_x, arrived_y = (
        lax.all_to_all(picked_x, "ep", split_axis=0, concat_axis=0, tiled=True),
        lax.all_to_all(picked_y, "ep", split_axis=0, concat_axis=0, tiled=True),
    )
    capacity = arrived_x.shape[0] * arrived_x.shape[1]
    arrived_x = arrived_x.reshape(capacity, -1)
    arrived_y = arrived_y.reshape(capacity, -1)
    full_x, full_y = (
        lax.all_gather(arrived_x, "et", axis=1, tiled=True),
        lax.all_gather(arrived_y, "et", axis=1, tiled=True),
    )
    w_first = w_up[0]
    w_second = w_down[0]
    pre_act = saved_pre[0]
    gate_row = gates[0]
    back_grad = lax.dot_general(
        full_y, w_second, (((1,), (1,)), ((), ())), preferred_element_type=jnp.float32
    )
    hidden = jnp.maximum(pre_act, jnp.zeros((), pre_act.dtype))
    expert_out = jnp.dot(hidden, w_second, preferred_element_type=jnp.float32)
    gate_term = jnp.sum(expert_out * full_y.astype(jnp.float32), axis=1)
    gate_total = lax.psum(gate_term, "et")
    pre_grad = (gate_row[:, None] * back_grad * (pre_act > 0)).astype(jnp.bfloat16)
    out_grad = (gate_row[:, None] * full_y.astype(jnp.float32)).astype(jnp.bfloat16)
    down_grad = lax.dot_general(
        hidden, out_grad, (((0,), (0,)), ((), ())), preferred_element_type=jnp.float32
    )
    up_grad = lax.dot_general(
        full_x, pre_grad, (((0,), (0,)), ((), ())), preferred_element_type=jnp.float32
    )
    positions = lax.broadcasted_iota(jnp.int32, (n_experts * n_slots, n_tokens), 1)
    selector = ((flat_idx[:, None] == positions) & slot_kept.reshape(-1)[:, None]).astype(
        jnp.float32
    )
    summed = lax.psum_scatter(
        lax.dot_general(
            w_first, pre_grad, (((1,), (1,)), ((), ())), preferred_element_type=jnp.float32
        ),
        "et",
        scatter_dimension=0,
        tiled=True,
    )
    returned = lax.all_to_all(summed, "ep", split_axis=1, concat_axis=1, tiled=True)
    token_grad = lax.dot_general(
        selector,
        returned,
        (((0,), (1,)), ((), ())),
        precision=lax.Precision.HIGHEST,
        preferred_element_type=jnp.float32,
    )
    return (
        token_grad.astype(jnp.bfloat16),
        up_grad.astype(jnp.bfloat16)[None],
        down_grad.astype(jnp.bfloat16)[None],
        gate_total[None],
    )


def solution(mesh):
    in_specs = (
        P("ep", "et"),
        P("ep", "et"),
        P("ep", None, "et"),
        P("ep", "et", None),
        P("ep", None, "et"),
        P("ep", None),
        P("ep", None, None),
        P("ep", None),
    )
    out_specs = (P("ep", "et"), P("ep", None, "et"), P("ep", "et", None), P("ep", None))
    return jax.shard_map(
        per_device, mesh=mesh, in_specs=in_specs, out_specs=out_specs, check_vma=False
    )
```

profile of v0, /device:TPU:8, one launch (start us, length us, event | category | flops | bytes accessed | tf_op | source)
XLA Modules:
  0.0 444.6 jit_solution(6837022788889596169)
XLA Ops:
  7.2 0.0 copy-start
  7.2 0.0 copy-start.3
  7.2 0.0 copy-start.2
  7.2 0.0 all-gather.3.cloned.1.call-start
  7.3 0.9 copy.12
  8.2 0.1 eq.10
  8.3 0.7 iota_compare_fusion.1
  9.0 1.9 gather_fusion.1
  10.9 1.9 gather_fusion
  12.8 0.1 broadcast_select_fusion
  13.0 0.1 broadcast_select_fusion.2
  13.1 22.0 %all_to_all.22 = bf16[32,16,128]{2,1,0:T(8,128)(2,1)} all-to-all(bf16[32,16,128]{2,1,0:T(8,128)(2,1)S(1)} %get-tuple-element.6), channel_id=1, replica_groups=mesh['ep'=32,'et'=16] {'ep'}, dimensions={0} | all-to-all | bytes 262144 | tf_op jit(solution)/shard_map/all_to_all | solution.py:20
  35.1 0.0 all-gather.3.cloned.1.call-update
  35.2 0.0 reduce-scatter.2.cloned.1.call-start
  35.2 86.2 %all-gather.3.cloned.1.call-done = bf16[512,2048]{1,0:T(8,128)(2,1)} async-done(((bf16[512,128]{1,0:T(8,128)(2,1)}), bf16[512,2048]{1,0:T(8,128)(2,1)}) %all-gather.3.cloned.1.call-update) | async-done | bytes 2097168 | tf_op jit(solution)/shard_map/all_gather | solution.py:27
  121.4 0.0 copy-done.3
  121.4 2.3 fusion.7
  123.8 2.7 convolution_bitcast_fusion
  126.5 0.0 reduce-scatter.2.cloned.1.call-update
  126.5 0.0 all-gather.5.cloned.1.call-start
  126.6 18.3 %all_to_all.23 = bf16[32,16,128]{2,1,0:T(8,128)(2,1)} all-to-all(bf16[32,16,128]{2,1,0:T(8,128)(2,1)S(1)} %get-tuple-element.5), channel_id=1, replica_groups=mesh['ep'=32,'et'=16] {'ep'}, dimensions={0} | all-to-all | bytes 262144 | tf_op jit(solution)/shard_map/all_to_all | solution.py:19
  144.8 0.0 all-gather.5.cloned.1.call-update
  144.9 0.1 lt.30
  144.9 2.1 fusion.1
  147.1 37.5 %psum.7 = f32[1,512]{1,0:T(1,128)} all-reduce(f32[1,512]{1,0:T(1,128)S(1)} %bitcast.41), channel_id=1, replica_groups=mesh['ep'=32,'et'=16] {'et'}, use_global_device_ids=true, to_apply=%region_2.4 | all-reduce | flops 512 | bytes 4096 | tf_op jit(solution)/shard_map/psum | solution.py:39
  184.6 155.6 %reduce-scatter.2.cloned.1.call-done = f32[128,512]{0,1:T(8,128)} async-done(((f32[2048,512]{0,1:T(8,128)}), f32[128,512]{0,1:T(8,128)}) %reduce-scatter.2.cloned.1.call-update) | async-done | bytes 262160 | tf_op jit(solution)/shard_map/reduce_scatter | solution.py:52
  340.2 7.8 %all-to-all-start.1 = ((f32[128,32,16]{0,2,1:T(8,128)}), f32[128,32,16]{0,2,1:T(8,128)S(1)}, u32[]{:S(2)}, u32[]{:S(2)}) async-start(f32[128,32,16]{0,2,1:T(8,128)} %bitcast.39), calls=%async_computation.2 | async-start | bytes 524288 | tf_op jit(solution)/shard_map/all_to_all | solution.py:60
  348.0 3.5 fusion.3
  351.4 81.9 %all-gather.5.cloned.1.call-done = bf16[512,2048]{1,0:T(8,128)(2,1)} async-done(((bf16[512,128]{1,0:T(8,128)(2,1)}), bf16[512,2048]{1,0:T(8,128)(2,1)}) %all-gather.5.cloned.1.call-update) | async-done | bytes 2097168 | tf_op jit(solution)/shard_map/all_gather | solution.py:26
  433.4 3.3 fusion.2
  436.7 0.0 all-to-all-done.1
  436.7 1.4 convolution_convert_fusion.2
  (9 shorter events, 0.0 us)
Async XLA Ops:
  7.2 116.6 %copy-start = (bf16[1,2048,256]{2,1,0:T(8,128)(2,1)S(1)}, bf16[1,2048,256]{2,1,0:T(8,128)(2,1)}, u32[]{:S(2)}) copy-start(bf16[1,2048,256]{2,1,0:T(8,128)(2,1)} %param.12) | copy-start | bytes 3145732
  7.2 114.2 %copy-start.3 = (bf16[1,512,256]{2,1,0:T(8,128)(2,1)S(1)}, bf16[1,512,256]{2,1,0:T(8,128)(2,1)}, u32[]{:S(2)}) copy-start(bf16[1,512,256]{2,1,0:T(8,128)(2,1)} %param.14) | copy-start | bytes 786436
  7.2 114.2 %copy-start.2 = (bf16[1,256,2048]{2,1,0:T(8,128)(2,1)S(1)}, bf16[1,256,2048]{2,1,0:T(8,128)(2,1)}, u32[]{:S(2)}) copy-start(bf16[1,256,2048]{2,1,0:T(8,128)(2,1)} %param.13) | copy-start | bytes 3145732
  7.2 114.2 %copy-start.4 = (f32[1,512]{1,0:T(1,128)S(1)}, f32[1,512]{1,0:T(1,128)}, u32[]{:S(2)}) copy-start(f32[1,512]{1,0:T(1,128)} %param.15) | copy-start | bytes 6148
  7.2 114.2 %all-gather.3.cloned.1.call-start = ((), (), s32[]{:S(2)}) async-start(), calls=%async_computation.4 | async-start | bytes 2228224 | tf_op jit(solution)/shard_map/all_gather | solution.py:27
  35.2 305.0 %reduce-scatter.2.cloned.1.call-start = ((), (), s32[]{:S(2)}) async-start(), calls=%async_computation.5 | async-start | bytes 4456448 | tf_op jit(solution)/shard_map/reduce_scatter | solution.py:52
  126.5 18.5 %copy-start.1 = (bf16[512,2048]{1,0:T(8,128)(2,1)S(1)}, bf16[512,2048]{1,0:T(8,128)(2,1)}, u32[]{:S(2)}) copy-start(bf16[512,2048]{1,0:T(8,128)(2,1)} %all-gather.3.cloned.1.call-done) | copy-start | bytes 6291460
  126.5 306.9 %all-gather.5.cloned.1.call-start = ((), (), s32[]{:S(2)}) async-start(), calls=%async_computation.6 | async-start | bytes 2228224 | tf_op jit(solution)/shard_map/all_gather | solution.py:26
  340.2 96.5 %all-to-all-start.1 = ((f32[128,32,16]{0,2,1:T(8,128)}), f32[128,32,16]{0,2,1:T(8,128)S(1)}, u32[]{:S(2)}, u32[]{:S(2)}) async-start(f32[128,32,16]{0,2,1:T(8,128)} %bitcast.39), calls=%async_computation.2 | async-start | bytes 524288 | tf_op jit(solution)/shard_map/all_to_all | solution.py:60
Sparse Core Ops, SparseCore 0:
  35.3 86.1 all-gather.2
  126.6 213.5 reduce-scatter.1
  343.7 89.6 all-gather.4
where the time goes:
time: 445 us
  waiting for transfers between devices  324 us (73%)
  blocking collectives  77.8 us (17%)
  matrix products  15.4 us (3%)
  between operations  13.8 us (3%)
  starting transfers between devices  7.89 us (2%)
  local copies, waits for them, and re-layouts  4.93 us (1%)
    reduce_scatter x1, waiting for transfers between devices, per_device(): lax.psum_scatter(lax.dot_general(w_first, pre_grad, (((1,), (1,)), ((), (...  156 us
    all_gather x1, waiting for transfers between devices, per_device(): lax.all_gather(arrived_y, 'et', axis=1, tiled=True)  86.2 us
    all_gather x1, waiting for transfers between devices, per_device(): lax.all_gather(arrived_x, 'et', axis=1, tiled=True)  81.9 us
    psum x1, blocking collectives, per_device(): gate_total = lax.psum(gate_term, 'et')  37.5 us
    all_to_all x1, blocking collectives, per_device(): lax.all_to_all(picked_y, 'ep', split_axis=0, concat_axis=0, tiled=True)  22 us
    all_to_all x1, blocking collectives, per_device(): lax.all_to_all(picked_x, 'ep', split_axis=0, concat_axis=0, tiled=True)  18.3 us
  transfers between devices with their start and end apart: 4, of which 3 were waited for; matrix products, arithmetic and copies ran while one was open for 2% of the time, Pallas kernels for 0%

commit v1 on v0

--- a/solution.py
+++ b/solution.py
@@ -24,7 +24,9 @@
     arrived_y = arrived_y.reshape(capacity, -1)
     full_x, full_y = (
         lax.all_gather(arrived_x, "et", axis=1, tiled=True),
-        lax.all_gather(arrived_y, "et", axis=1, tiled=True),
+        jnp.concatenate(
+            lax.all_to_all(jnp.stack([arrived_y] * lax.axis_size("et")), "et", 0, 0), axis=1
+        ),
     )
     w_first = w_up[0]
     w_second = w_down[0]

time: 445 us -> 413 us (0.928)
  waiting for transfers between devices: 324 us -> 233 us
  blocking collectives: 77.8 us -> 132 us
    all_gather x1 -> x0, waiting for transfers between devices: 86.2 us -> none  [per_device(): lax.all_gather(arrived_y, 'et', axis=1, tiled=True)]
    all_to_all x0 -> x1, blocking collectives: none -> 58.7 us  [per_device(): lax.all_to_all(jnp.stack([arrived_y] * lax.axis_size('et')), 'et', 0, 0)]
    reduce_scatter x1, waiting for transfers between devices: 156 us -> 151 us  [per_device(): lax.psum_scatter(lax.dot_general(w_first, pre_grad, (((1,), (1,)), ((), (...]
  transfers between devices with their start and end apart: 4 -> 3, of which waited for: 3 -> 2; matrix products, arithmetic and copies ran while one was open for 2% -> 3% of each run, Pallas kernels for 0% -> 0%
where the time goes in v1:
time: 413 us; the launch traced here: 412 us
  waiting for transfers between devices  233 us (56%)
  blocking collectives  132 us (32%)
  between operations  14.2 us (3%)
  matrix products  12.9 us (3%)
  local copies, waits for them, and re-layouts  8.6 us (2%)
  starting transfers between devices  7.86 us (2%)
    reduce_scatter x1, waiting for transfers between devices, per_device(): lax.psum_scatter(lax.dot_general(w_first, pre_grad, (((1,), (1,)), ((), (...  151 us
    all_gather x1, waiting for transfers between devices, per_device(): lax.all_gather(arrived_x, 'et', axis=1, tiled=True)  82.7 us
    all_to_all x1, blocking collectives, per_device(): lax.all_to_all(jnp.stack([arrived_y] * lax.axis_size('et')), 'et', 0, 0)  58.7 us
    psum x1, blocking collectives, per_device(): gate_total = lax.psum(gate_term, 'et')  37.7 us
    all_to_all x1, blocking collectives, per_device(): lax.all_to_all(picked_y, 'ep', split_axis=0, concat_axis=0, tiled=True)  21.9 us
    all_to_all x1, blocking collectives, per_device(): lax.all_to_all(picked_x, 'ep', split_axis=0, concat_axis=0, tiled=True)  14.1 us
  transfers between devices with their start and end apart: 3, of which 2 were waited for; matrix products, arithmetic and copies ran while one was open for 3% of the time, Pallas kernels for 0%

profile of v1, /device:TPU:8, one launch (start us, length us, event | category | flops | bytes accessed | tf_op | source)
XLA Modules:
  0.0 412.3 jit_solution(10228927172980398042)
XLA Ops:
  7.2 0.0 copy-start
  7.2 0.0 reduce-scatter.2.cloned.1.call-start
  7.2 0.8 copy.15
  8.1 0.1 eq.10
  8.2 0.7 iota_compare_fusion.1
  8.9 1.9 gather_fusion.1
  10.8 1.9 gather_fusion
  12.7 0.1 broadcast_select_fusion
  12.9 0.1 broadcast_select_fusion.2
  13.0 21.9 %all_to_all.27 = bf16[32,16,128]{2,1,0:T(8,128)(2,1)S(1)} all-to-all(bf16[32,16,128]{2,1,0:T(8,128)(2,1)S(1)} %get-tuple-element.6), channel_id=1, replica_groups=mesh['ep'=32,'et'=16] {'ep'}, dimensions={0} | all-to-all | bytes 262144 | tf_op jit(solution)/shard_map/all_to_all | solution.py:20
  34.9 0.4 stack.3
  35.3 0.0 copy-start.3
  35.3 0.0 copy-start.4
  35.4 58.7 %all_to_all.28 = bf16[16,512,128]{2,1,0:T(8,128)(2,1)S(1)} all-to-all(bf16[16,512,128]{2,1,0:T(8,128)(2,1)S(1)} %stack.3), channel_id=1, replica_groups=mesh['ep'=32,'et'=16] {'et'}, dimensions={0} | all-to-all | bytes 4194304 | tf_op jit(solution)/shard_map/all_to_all | solution.py:28
  94.1 0.8 fusion.11
  94.9 0.7 copy-done.2
  95.6 2.7 convolution_bitcast_fusion
  98.3 0.0 reduce-scatter.2.cloned.1.call-update
  98.3 0.0 all-gather.2.cloned.1.call-start
  98.3 14.1 %all_to_all.29 = bf16[32,16,128]{2,1,0:T(8,128)(2,1)} all-to-all(bf16[32,16,128]{2,1,0:T(8,128)(2,1)S(1)} %get-tuple-element.5), channel_id=1, replica_groups=mesh['ep'=32,'et'=16] {'ep'}, dimensions={0} | all-to-all | bytes 262144 | tf_op jit(solution)/shard_map/all_to_all | solution.py:19
  112.5 0.0 all-gather.2.cloned.1.call-update
  112.5 0.1 lt.30
  112.6 2.6 copy.16
  115.2 2.0 multiply_reduce_fusion
  117.2 37.7 %psum.7 = f32[1,512]{1,0:T(1,128)} all-reduce(f32[1,512]{1,0:T(1,128)S(1)} %bitcast.64), channel_id=1, replica_groups=mesh['ep'=32,'et'=16] {'et'}, use_global_device_ids=true, to_apply=%region_2.4 | all-reduce | flops 512 | bytes 4096 | tf_op jit(solution)/shard_map/psum | solution.py:41
  154.9 2.1 multiply_convert_fusion
  157.0 150.6 %reduce-scatter.2.cloned.1.call-done = f32[128,512]{0,1:T(8,128)} async-done(((f32[2048,512]{0,1:T(8,128)}), f32[128,512]{0,1:T(8,128)}) %reduce-scatter.2.cloned.1.call-update) | async-done | bytes 262160 | tf_op jit(solution)/shard_map/reduce_scatter | solution.py:54
  307.6 7.8 %all-to-all-start.2 = ((f32[128,32,16]{0,2,1:T(8,128)}), f32[128,32,16]{0,2,1:T(8,128)S(1)}, u32[]{:S(2)}, u32[]{:S(2)}) async-start(f32[128,32,16]{0,2,1:T(8,128)} %bitcast.60), calls=%async_computation.3 | async-start | bytes 524288 | tf_op jit(solution)/shard_map/all_to_all | solution.py:62
  315.4 2.7 fusion.1
  318.1 82.7 %all-gather.2.cloned.1.call-done = bf16[512,2048]{1,0:T(8,128)(2,1)} async-done(((bf16[512,128]{1,0:T(8,128)(2,1)}), bf16[512,2048]{1,0:T(8,128)(2,1)}) %all-gather.2.cloned.1.call-update) | async-done | bytes 2097168 | tf_op jit(solution)/shard_map/all_gather | solution.py:26
  400.8 3.3 fusion
  404.1 1.4 convolution_convert_fusion.2
  (10 shorter events, 0.0 us)
Async XLA Ops:
  7.2 88.4 %copy-start = (bf16[1,2048,256]{2,1,0:T(8,128)(2,1)S(1)}, bf16[1,2048,256]{2,1,0:T(8,128)(2,1)}, u32[]{:S(2)}) copy-start(bf16[1,2048,256]{2,1,0:T(8,128)(2,1)} %param.12) | copy-start | bytes 3145732
  7.2 300.4 %reduce-scatter.2.cloned.1.call-start = ((), (), s32[]{:S(2)}) async-start(), calls=%async_computation.5 | async-start | bytes 4456448 | tf_op jit(solution)/shard_map/reduce_scatter | solution.py:54
  35.3 58.8 %copy-start.1 = (bf16[1,512,256]{2,1,0:T(8,128)(2,1)S(1)}, bf16[1,512,256]{2,1,0:T(8,128)(2,1)}, u32[]{:S(2)}) copy-start(bf16[1,512,256]{2,1,0:T(8,128)(2,1)} %param.14) | copy-start | bytes 786436
  35.3 58.8 %copy-start.3 = (f32[1,512]{1,0:T(1,128)S(1)}, f32[1,512]{1,0:T(1,128)}, u32[]{:S(2)}) copy-start(f32[1,512]{1,0:T(1,128)} %param.15) | copy-start | bytes 6148
  35.3 58.8 %copy-start.4 = (bf16[1,256,2048]{2,1,0:T(8,128)(2,1)S(1)}, bf16[1,256,2048]{2,1,0:T(8,128)(2,1)}, u32[]{:S(2)}) copy-start(bf16[1,256,2048]{2,1,0:T(8,128)(2,1)} %param.13) | copy-start | bytes 3145732
  94.9 0.7 copy-start.2
  98.3 302.5 %all-gather.2.cloned.1.call-start = ((), (), s32[]{:S(2)}) async-start(), calls=%async_computation.6 | async-start | bytes 2228224 | tf_op jit(solution)/shard_map/all_gather | solution.py:26
  307.6 96.5 %all-to-all-start.2 = ((f32[128,32,16]{0,2,1:T(8,128)}), f32[128,32,16]{0,2,1:T(8,128)S(1)}, u32[]{:S(2)}, u32[]{:S(2)}) async-start(f32[128,32,16]{0,2,1:T(8,128)} %bitcast.60), calls=%async_computation.3 | async-start | bytes 524288 | tf_op jit(solution)/shard_map/all_to_all | solution.py:62
Sparse Core Ops, SparseCore 0:
  98.4 209.1 reduce-scatter.1
  311.1 89.6 all-gather.1
